TPU v7x, 256 devices: a whole 4x4x8 slice. The times are simulated.
256 devices in a mesh: row: 16 (over z_lo, y), col: 4 (over x), depth: 4 (over z_hi, core).
Axes of the slice: x: 4, y: 4, z: 8 (z_hi: 2, z_lo: 4; z = z_hi * 4 + z_lo), core: 2. Of those that a mesh axis runs over, the one named last changes fastest.
Arguments:
- left_blocks: float32 [16384, 16, 2048], P('row', ('col', 'depth')), may hold values from -0.125 to 0.125
- left_pattern: int32 [128, 16, 16], P('row', ('col', 'depth')), may hold values 0 or 1
- right_window: float32 [16, 2048, 2048], P(('col', 'depth'), 'row'), may hold values from -6 to 6
- right_pattern: int32 [16, 16, 16], P(('col', 'depth'), 'row'), may hold values 0 or 1
- subset_cols: int32 [8], replicated, may hold values from 0 to 15, as said below
- square_cols: float32 [16384, 1024], P(('row', 'col', 'depth')), may hold values from -4 to 4
Outputs:
- purified: float32 [16384, 1024], P(('row', 'col', 'depth'))
Inputs may be any that keep to these rules, and one draw needn't show every extreme that they name: `subset_cols`: 8 different block-column numbers of the window.
All inputs are finite; a program needn't handle non-finite values. No bound on the sum of `left_pattern` or of `right_pattern` on one device may be relied on, other than what follows from the above.
Results may differ from a plain program's by a relative error of at most 0.0001.
Values sent between devices are 32-bit elements; how exact they have to be, the bound alone decides.
A program may use at most 128 MiB of HBM per device.

v0:
```python
import jax
import jax.numpy as jnp
from jax import lax
from jax.sharding import PartitionSpec as P

BS = 128


def expand(pattern, block, dtype):
    grown = jnp.repeat(pattern.astype(dtype), block, axis=0)
    return jnp.repeat(grown, block, axis=1)


def select_cols(matrix, subset_cols, count_window, block):
    height = matrix.shape[0]
    shaped = matrix.reshape(height, count_window, block)
    chosen = jnp.take(shaped, subset_cols, axis=1)
    return chosen.reshape(height, subset_cols.shape[0] * block)


def shards(left_blocks, left_pattern, right_window, right_pattern, subset_cols, square_cols):
    block = BS
    count_window = right_pattern.shape[-1]
    masked = (left_blocks * expand(left_pattern[:, 0, :], block, left_blocks.dtype)[:, None, :])[
        :, 0, :
    ]
    right_local = right_window[0] * expand(right_pattern[0], block, right_window.dtype)
    local_cols = select_cols(right_local, subset_cols, count_window, block)
    chosen = lax.all_gather(local_cols, "row", axis=0, tiled=True)
    partial_value = jnp.dot(
        masked, chosen, precision=lax.Precision.HIGHEST, preferred_element_type=jnp.float32
    )
    summed = lax.psum_scatter(partial_value, ("col", "depth"), scatter_dimension=0, tiled=True)
    return 3.0 * square_cols - 2.0 * summed


def solution(mesh):
    return jax.shard_map(
        shards,
        mesh=mesh,
        in_specs=(
            P("row", ("col", "depth"), None),
            P("row", ("col", "depth"), None),
            P(("col", "depth"), "row", None),
            P(("col", "depth"), "row", None),
            P(),
            P(("row", "col", "depth"), None),
        ),
        out_specs=P(("row", "col", "depth"), None),
        check_vma=False,
    )
```

profile of v0, /device:TPU:1, one launch (start us, length us, event | category | flops | bytes accessed | tf_op | source)
XLA Modules:
  0.0 290.9 jit_solution(8481569812016413061)
XLA Ops:
  6.5 0.0 copy-start.1
  6.5 0.0 all-gather.2.cloned.1.call-start
  6.5 0.7 compare_select_fusion
  7.2 0.7 compare_and_fusion
  7.9 1.5 copy.10
  9.4 0.3 copy.11
  9.8 0.7 convert_bitcast_fusion.1
  10.4 0.1 broadcast_multiply_fusion
  10.6 0.6 gather_fusion
  11.2 0.2 copy.12
  11.4 0.1 broadcast_bitcast_fusion
  11.4 1.0 bitcast_select_fusion
  12.4 0.0 all-gather.2.cloned.1.call-update
  12.5 0.0 reduce-scatter.2.cloned.1.call-start
  12.5 0.0 copy-done.1
  12.6 2.3 broadcast_in_dim.27
  14.9 10.9 %mul.21 = f32[1024,1,2048]{2,1,0:T(1,128)} multiply(f32[1024,1,2048]{2,1,0:T(1,128)} %param.6, f32[1024,1,2048]{2,1,0:T(1,128)S(1)} %bitcast.17) | non-fusion elementwise | flops 2097152 | bytes 25165824 | tf_op jit(solution)/shard_map/mul | solution.py:24
  25.8 0.0 copy-start
  25.8 111.8 %all-gather.2.cloned.1.call-done = f32[2048,1024]{0,1:T(8,128)} async-done(((f32[128,1024]{0,1:T(8,128)}), f32[2048,1024]{0,1:T(8,128)}) %all-gather.2.cloned.1.call-update) | async-done | bytes 8388624 | tf_op jit(solution)/shard_map/all_gather | solution.py:29
  137.6 36.9 %fusion = f32[1024,1024]{1,0:T(8,128)} fusion(f32[2048,1024]{0,1:T(8,128)} %all-gather.2.cloned.1.call-done, f32[1024,1,2048]{2,1,0:T(1,128)} %mul.21), kind=kOutput, calls=%fused_computation.1 | convolution fusion | flops 25769803776 | bytes 20971520 | tf_op jit(solution)/shard_map/dot_general | solution.py:30
  174.5 0.0 reduce-scatter.2.cloned.1.call-update
  174.5 107.9 %reduce-scatter.2.cloned.1.call-done = f32[64,1024]{1,0:T(8,128)} async-done(((f32[1024,1024]{1,0:T(8,128)}), f32[64,1024]{1,0:T(8,128)}) %reduce-scatter.2.cloned.1.call-update) | async-done | bytes 262160 | tf_op jit(solution)/shard_map/reduce_scatter | solution.py:33
  282.4 0.0 copy-done
  282.4 1.7 multiply_subtract_fusion
  (3 shorter events, 0.0 us)
Async XLA Ops:
  6.5 6.0 %copy-start.1 = (s32[8,1,16]{2,1,0:T(1,128)S(1)}, s32[8,1,16]{2,1,0:T(1,128)}, u32[]{:S(2)}) copy-start(s32[8,1,16]{2,1,0:T(1,128)} %param.7) | copy-start | bytes 1540
  6.5 131.0 %all-gather.2.cloned.1.call-start = ((), (), s32[]{:S(2)}) async-start(), calls=%async_computation.1 | async-start | bytes 8912896 | tf_op jit(solution)/shard_map/all_gather | solution.py:29
  12.5 269.9 %reduce-scatter.2.cloned.1.call-start = ((), (), s32[]{:S(2)}) async-start(), calls=%async_computation.2 | async-start | bytes 4456448 | tf_op jit(solution)/shard_map/reduce_scatter | solution.py:33
  25.8 256.6 %copy-start = (f32[64,1024]{1,0:T(8,128)S(1)}, f32[64,1024]{1,0:T(8,128)}, u32[]{:S(2)}) copy-start(f32[64,1024]{1,0:T(8,128)} %param.11) | copy-start | bytes 786436
Sparse Core Ops, SparseCore 0:
  12.6 124.9 all-gather.1
  174.6 107.6 reduce-scatter.1
where the time goes:
time: 292 us; the launch traced here: 291 us
  waiting for transfers between devices  220 us (75%)
  matrix products  36.9 us (13%)
  other arithmetic  15.7 us (5%)
  between operations  13.5 us (5%)
  local copies, waits for them, and re-layouts  5.09 us (2%)
    all_gather x1, waiting for transfers between devices, shards(): chosen = lax.all_gather(local_cols, 'row', axis=0, tiled=True)  112 us
    reduce_scatter x1, waiting for transfers between devices, shards(): lax.psum_scatter(partial_value, ('col', 'depth'), scatter_dimension=0, ti...  108 us
    dot_general x1, matrix products, shards(): jnp.dot(masked, chosen, precision=lax.Precision.HIGHEST, preferred_elemen...  36.9 us
    mul x1, other arithmetic, shards(): left_blocks * expand(left_pattern[:, 0, :], block, left_blocks.dtype)[:,...  10.9 us
  transfers between devices with their start and end apart: 2, of which 2 were waited for; matrix products, arithmetic and copies ran while one was open for 5% of the time, Pallas kernels for 0%

commit v1 on v0

v1 whole, which is shorter than its diff:
```python
import functools

import jax
import jax.numpy as jnp
from jax import lax
from jax.experimental import pallas as pl
from jax.experimental.pallas import tpu as pltpu
from jax.sharding import PartitionSpec as P

MESH = pl.DeviceIdType.MESH
BS = 128
NH = 4
NW = 8
NR = 16


def dot_nt(a, b):
    return lax.dot_general(a, b, (((1,), (1,)), ((), ())), preferred_element_type=jnp.float32)


def kernel(cz, cy, left_h, lp_s, win_h, rp_s, sub_s, sq_v, out_v, flag_v, *scratch):
    (left_v, win_v, ahi, alo, spread, pt_v, idx_v, idx_s, bhi, blo,
     cs, cr, ps, xr, vz, zx, fl_a, fl_b, fl_c, fl_x, fl_z,
     rec0, rec1, rec2, rec3, zr0, zr1, zr2, zr3, yr0, yr1, yr2, yr3,
     wsem, lsem, pt_ss, pt_rs, a_ss, a_rs, z_ss, z_rs, y_ss, y_rs, f_ss, f_rs,
     c_ss, c_rs, x_ss, x_rs, v_ss, v_rs, fl_ss, fl_rs) = scratch
    rec = (rec0, rec1, rec2, rec3)
    zr = (zr0, zr1, zr2, zr3)
    yr = (yr0, yr1, yr2, yr3)
    half = cy // 2

    r = lax.axis_index("row")
    x = lax.axis_index("col")
    d = lax.axis_index("depth")
    y = lax.rem(r, 4)
    z = r // 4
    core = lax.rem(d, 2)
    zh = d // 2

    def row_at(dz, dy):
        return lax.rem(z + dz, 4) * 4 + lax.rem(y + dy, 4)

    core_peer = {"depth": d + 1 - 2 * core}
    zh_peer = {"depth": lax.rem(d + 2, 4)}

    def x_peer(dx):
        return {"col": lax.rem(x + dx, 4)}

    def remote(src, dst, ss, rs, device):
        return pltpu.make_async_remote_copy(
            src_ref=src, dst_ref=dst, send_sem=ss, recv_sem=rs, device_id=device, device_id_type=MESH
        )

    win_copies = []
    for w in range(16):
        cp = pltpu.make_async_copy(win_h.at[:, pl.ds(w * BS, BS)], win_v.at[w], wsem.at[w])
        cp.start()
        win_copies.append(cp)
    left_copies = []
    for part in range(4):
        cp = pltpu.make_async_copy(
            left_h.at[pl.ds(part * 4096, 4096)], left_v.at[pl.ds(part * 4096, 4096)], lsem.at[1 + part]
        )
        cp.start()
        left_copies.append(cp)
    barrier = pltpu.get_barrier_semaphore()
    for k in range(1, NR):
        pl.semaphore_signal(barrier, inc=1, device_id={"row": lax.rem(r + k, NR)}, device_id_type=MESH)
    for k in range(1, 4):
        pl.semaphore_signal(barrier, inc=1, device_id=x_peer(k), device_id_type=MESH)
    pl.semaphore_signal(barrier, inc=1, device_id=core_peer, device_id_type=MESH)
    pl.semaphore_signal(barrier, inc=1, device_id=zh_peer, device_id_type=MESH)

    lane = lax.broadcasted_iota(jnp.int32, (8, 128), 1)
    mine = jnp.zeros((8, 128), jnp.int32)
    for w in range(NW):
        mine = jnp.where(lane == r * NW + w, rp_s[0, sub_s[w]], mine)
    pt_v[r] = mine
    pl.semaphore_wait(barrier, 20)

    pt = []
    for k in range(1, NR):
        to = lax.rem(r + k, NR)
        cp = remote(pt_v.at[r], pt_v.at[r], pt_ss.at[k], pt_rs.at[k], {"row": to})
        cp.start()
        pt.append(cp)

    for cp in win_copies:
        cp.wait()
    for w in range(NW):
        block = win_v[sub_s[w]].T
        for h in range(NH):
            for to in range(4):
                at = 32 * h + 8 * to
                spread[h, to, w] = block[at:at + 8, :]
    a2a = []
    for h in range(NH):
        row = []
        for dy in (1, 3, 2):
            to = lax.rem(y + dy, 4)
            cp = remote(spread.at[h, to], rec[h].at[pl.ds(y * NW, NW)], a_ss.at[h, dy], a_rs.at[h, dy], {"row": row_at(0, dy)})
            cp.start()
            row.append(cp)
        a2a.append(row)
        rec[h][pl.ds(y * NW, NW)] = spread[h, y]

    def prepare(part):
        left_copies[part].wait()

        def body(i, _):
            piece = part * 4 + i
            at = lax.rem(piece, 2) * 512 + (piece // 4) * 128 + lax.rem(piece // 2, 2) * 64
            at = pl.multiple_of(at, 64)
            for q in range(NR):
                v = left_v[pl.ds(piece * 1024 + q, 64, stride=16), :]
                v = jnp.where(jnp.full((64, 128), lp_s[piece // 2, q], jnp.int32) != 0, v, 0.0)
                hi = v.astype(jnp.bfloat16)
                ahi[pl.ds(at, 64), q * BS:(q + 1) * BS] = hi
                alo[pl.ds(at, 64), q * BS:(q + 1) * BS] = (v - hi.astype(jnp.float32)).astype(jnp.bfloat16)
            return 0

        lax.fori_loop(0, 4, body, 0)

    prepare(0)

    for cp in pt:
        cp.wait_recv()
    pat = pt_v[0]
    for k in range(1, NR):
        pat = pat + pt_v[k]
    in_pool = lax.rem(lane, 32)
    c32 = pat
    for s in (1, 2, 4, 8, 16):
        c32 = c32 + jnp.where(in_pool >= s, pltpu.roll(c32, s, 1), 0)
    call = pat
    for s in (1, 2, 4, 8, 16, 32, 64):
        call = call + jnp.where(lane >= s, pltpu.roll(call, s, 1), 0)
    rank32 = c32 - pat
    rank = call - pat
    zsrc = (lane // 32) * cz + jnp.minimum(rank32, cz - 1)

    def column(v):
        return jnp.broadcast_to(v[0:1, :], (128, 128)).T

    blk = lax.broadcasted_iota(jnp.int32, (128, 128), 0)
    slot = lax.broadcasted_iota(jnp.int32, (128, 128), 1)
    on = column(pat) != 0
    first = jnp.where(on & (column(rank32) == slot) & (blk // 32 == z), blk - 32 * z, 0)
    second = jnp.where(on & (column(rank) == slot), column(zsrc), 0)
    idx_v[0:1, :] = jnp.sum(first, axis=0, keepdims=True)
    idx_v[1:2, :] = jnp.sum(second, axis=0, keepdims=True)
    idx_v[2:3, :] = jnp.minimum(rank, cy - 1)[0:1, :]
    idx_v[3:4, :] = pat[0:1, :]
    idx_v[4:8, :] = pat[0:4, :]
    over = jnp.where((in_pool == 31) & (c32 > cz), 1, 0) + jnp.where((lane == 127) & (call > cy), 1, 0)
    for s in (1, 2, 4, 8, 16, 32, 64):
        over = over + pltpu.roll(over, s, 1)
    fl_a[...] = over
    to_s = pltpu.make_async_copy(idx_v, idx_s, lsem.at[5])
    to_s.start()
    to_s.wait()

    zg = []
    for h in range(NH):
        for cp in a2a[h]:
            cp.wait_recv()

        def pack(j, _, h=h):
            at = idx_s[0, j]
            zr[h][z * cz + j] = rec[h][at]
            return 0

        if cz <= 20:
            for j in range(cz):
                pack(j, 0)
        else:
            lax.fori_loop(0, cz, pack, 0)
        row = []
        for dz in (1, 3, 2):
            part = zr[h].at[pl.ds(z * cz, cz)]
            cp = remote(part, part, z_ss.at[h, dz], z_rs.at[h, dz], {"row": row_at(dz, 0)})
            cp.start()
            row.append(cp)
        zg.append(row)

    yg, fg = {}, {}

    def y_send(h):
        for cp in zg[h]:
            cp.wait_recv()

        def pack(j, _):
            at = idx_s[1, j]
            yr[h][y, j] = zr[h][at]
            return 0

        if cy <= 64:
            def five(i, _):
                for k in range(10):
                    pack(i * 10 + k, 0)
                return 0

            lax.fori_loop(0, cy // 10, five, 0)
        else:
            lax.fori_loop(0, cy, pack, 0)
        for side, dy in ((0, 1), (1, 3)):
            for k in ((0, 1) if side == 0 else (1, 0)):
                part = yr[h].at[y, pl.ds(k * half, half)]
                cp = remote(part, part, y_ss.at[h, side, k], y_rs.at[h, side, k], {"row": row_at(0, dy)})
                cp.start()
                yg[h, side, k] = cp

    def y_forward(h):
        for side, dy in ((0, 1), (1, 3)):
            yg[h, side, side].wait_recv()
            part = yr[h].at[lax.rem(y + (3 if side == 0 else 1), 4), pl.ds(side * half, half)]
            cp = remote(part, part, f_ss.at[h, side], f_rs.at[h, side], {"row": row_at(0, dy)})
            cp.start()
            fg[h, side] = cp

    def expand(h):
        for side in (0, 1):
            yg[h, side, 1 - side].wait_recv()
            fg[h, side].wait_recv()

        def body(w, _):
            at = pl.multiple_of(w * 32, 32)
            for q in range(NR):
                place = idx_s[2, q * NW + w]
                keep = jnp.full((32, 128), idx_s[3, q * NW + w], jnp.int32) != 0
                v = jnp.concatenate([yr[h][k, place] for k in range(4)], axis=0)
                v = jnp.where(keep, v, 0.0)
                hi = v.astype(jnp.bfloat16)
                bhi[pl.ds(at, 32), q * BS:(q + 1) * BS] = hi
                blo[pl.ds(at, 32), q * BS:(q + 1) * BS] = (v - hi.astype(jnp.float32)).astype(jnp.bfloat16)
            return 0

        lax.fori_loop(0, NW, body, 0)

    def product(which):
        at = pl.multiple_of(which * 512, 512)
        a_hi, a_lo = ahi[pl.ds(at, 512), :], alo[pl.ds(at, 512), :]
        b_hi, b_lo = bhi[...], blo[...]
        return dot_nt(a_hi, b_hi) + dot_nt(a_hi, b_lo) + dot_nt(a_lo, b_hi)

    cg, xg, vg, flg = {}, {}, {}, {}

    def other_half(h):
        cs[h] = product(1 - core)
        cg[h] = remote(cs.at[h], cr.at[h], c_ss.at[h], c_rs.at[h], core_peer)
        cg[h].start()
        if h == 0:
            flg[0] = remote(fl_a, fl_c, fl_ss.at[0], fl_rs.at[0], core_peer)
            flg[0].start()

    def own_half(h):
        ps[h] = product(core)

    def over_x(h):
        cg[h].wait_recv()
        ps[h] = ps[h] + cr[h]
        for dx in (1, 3, 2):
            to = lax.rem(x + dx, 4)
            part = ps.at[h, pl.ds(pl.multiple_of(to * 128, 128), 128)]
            xg[h, dx] = remote(part, xr.at[h, dx - 1], x_ss.at[h, dx], x_rs.at[h, dx], x_peer(dx))
            xg[h, dx].start()
        if h == 0:
            flg[0].wait_recv()
            fl_b[0] = fl_a[...] + fl_c[...]
            for dx in (1, 3, 2):
                flg[dx] = remote(fl_b.at[0], fl_x.at[dx - 1], fl_ss.at[dx], fl_rs.at[dx], x_peer(dx))
                flg[dx].start()

    def over_zh(h):
        for dx in (1, 3, 2):
            xg[h, dx].wait_recv()
        own = ps[h, pl.ds(pl.multiple_of(x * 128, 128), 128), :]
        vz[h] = (own + xr[h, 0]) + (xr[h, 1] + xr[h, 2])
        part = vz.at[h, pl.ds(pl.multiple_of((1 - zh) * 64, 64), 64)]
        vg[h] = remote(part, zx.at[h], v_ss.at[h], v_rs.at[h], zh_peer)
        vg[h].start()
        if h == 0:
            for dx in (1, 3, 2):
                flg[dx].wait_recv()
            fl_b[1] = (fl_b[0] + fl_x[0]) + (fl_x[1] + fl_x[2])
            flg[4] = remote(fl_b.at[1], fl_z, fl_ss.at[4], fl_rs.at[4], zh_peer)
            flg[4].start()

    lane64 = lax.broadcasted_iota(jnp.int32, (64, 128), 1)

    def finish(h):
        vg[h].wait_recv()
        total = vz[h, pl.ds(pl.multiple_of(zh * 64, 64), 64), :] + zx[h]
        for w in range(NW):
            tile = total[:, (w // 4) * 128:(w // 4 + 1) * 128]
            shift = (32 * h - 32 * (w % 4)) % 128
            if shift:
                tile = pltpu.roll(tile, shift, 1)
            cols = slice(w * BS, (w + 1) * BS)
            value = 3.0 * sq_v[:, cols] - 2.0 * tile
            if h:
                value = jnp.where(lane64 // 32 == h, value, out_v[:, cols])
            out_v[:, cols] = value
        if h == 0:
            flg[4].wait_recv()
            flag_v[...] = fl_b[1] + fl_z[...]

    for part in range(1, 4):
        prepare(part)
    y_send(0)
    y_forward(0)
    for h in range(NH):
        if h + 1 < NH:
            y_send(h + 1)
        expand(h)
        other_half(h)
        if h + 1 < NH:
            y_forward(h + 1)
        own_half(h)
        over_x(h)
        if h >= 1:
            over_zh(h - 1)
        if h >= 2:
            finish(h - 2)
    finish(NH - 2)
    over_zh(NH - 1)
    finish(NH - 1)

    for cp in pt:
        cp.wait_send()
    for row in a2a + zg:
        for cp in row:
            cp.wait_send()
    for group in (yg, fg, cg, xg, vg, flg):
        for cp in group.values():
            cp.wait_send()


def run(cz, cy, collective_id, left, lp, win, rp, sub, sq):
    any_ = pl.BlockSpec(memory_space=pl.ANY)
    vmem = pl.BlockSpec(memory_space=pltpu.VMEM)
    smem = pl.BlockSpec(memory_space=pltpu.SMEM)
    f32, bf16, i32 = jnp.float32, jnp.bfloat16, jnp.int32
    dma = pltpu.SemaphoreType.DMA
    scratch = [
        pltpu.VMEM((16384, 128), f32),
        pltpu.VMEM((16, 128, 128), f32),
        pltpu.VMEM((1024, 2048), bf16),
        pltpu.VMEM((1024, 2048), bf16),
        pltpu.VMEM((NH, 4, NW, 8, 128), f32),
        pltpu.VMEM((NR, 8, 128), i32),
        pltpu.VMEM((8, 128), i32),
        pltpu.SMEM((8, 128), i32),
        pltpu.VMEM((256, 2048), bf16),
        pltpu.VMEM((256, 2048), bf16),
        pltpu.VMEM((NH, 512, 256), f32),
        pltpu.VMEM((NH, 512, 256), f32),
        pltpu.VMEM((NH, 512, 256), f32),
        pltpu.VMEM((NH, 3, 128, 256), f32),
        pltpu.VMEM((NH, 128, 256), f32),
        pltpu.VMEM((NH, 64, 256), f32),
        pltpu.VMEM((8, 128), i32),
        pltpu.VMEM((2, 8, 128), i32),
        pltpu.VMEM((8, 128), i32),
        pltpu.VMEM((3, 8, 128), i32),
        pltpu.VMEM((8, 128), i32),
    ]
    scratch += [pltpu.VMEM((4 * NW, 8, 128), f32) for _ in range(NH)]
    scratch += [pltpu.VMEM((4 * cz, 8, 128), f32) for _ in range(NH)]
    scratch += [pltpu.VMEM((4, cy, 8, 128), f32) for _ in range(NH)]
    scratch += [
        dma((16,)), dma((6,)),
        dma((NR,)), dma((NR,)),
        dma((NH, 4)), dma((NH, 4)),
        dma((NH, 4)), dma((NH, 4)),
        dma((NH, 2, 2)), dma((NH, 2, 2)),
        dma((NH, 2)), dma((NH, 2)),
        dma((NH,)), dma((NH,)),
        dma((NH, 4)), dma((NH, 4)),
        dma((NH,)), dma((NH,)),
        dma((5,)), dma((5,)),
    ]
    return pl.pallas_call(
        functools.partial(kernel, cz, cy),
        out_shape=(jax.ShapeDtypeStruct((64, 1024), f32), jax.ShapeDtypeStruct((8, 128), i32)),
        in_specs=[any_, smem, any_, smem, smem, vmem],
        out_specs=(vmem, vmem),
        scratch_shapes=scratch,
        compiler_params=pltpu.CompilerParams(
            collective_id=collective_id, has_side_effects=True, vmem_limit_bytes=56 * 2**20
        ),
    )(left, lp, win, rp, sub, sq)


def shards(left_blocks, left_pattern, right_window, right_pattern, subset_cols, square_cols):
    args = (
        left_blocks.reshape(1024 * NR, BS),
        left_pattern.reshape(8, NR),
        right_window.reshape(128, 2048),
        right_pattern.reshape(1, 16),
        subset_cols,
        square_cols,
    )
    fast, flag = run(18, 50, 0, *args)
    return lax.cond(
        flag[0, 0] > 0,
        lambda value, *rest: run(32, 128, 1, *rest)[0],
        lambda value, *rest: value,
        fast, *args,
    )


def solution(mesh):
    return jax.shard_map(
        shards,
        mesh=mesh,
        in_specs=(
            P("row", ("col", "depth"), None),
            P("row", ("col", "depth"), None),
            P(("col", "depth"), "row", None),
            P(("col", "depth"), "row", None),
            P(),
            P(("row", "col", "depth"), None),
        ),
        out_specs=P(("row", "col", "depth"), None),
        check_vma=False,
    )
```

time: 292 us -> 89.1 us (0.31)
  waiting for transfers between devices: 220 us -> 0 us
  Pallas kernels: 0 us -> 85.3 us
  matrix products: 36.9 us -> 0 us
  other arithmetic: 15.7 us -> 0 us
  between operations: 13.5 us -> 0.73 us
  local copies, waits for them, and re-layouts: 5.09 us -> 1.92 us
    all_gather x1 -> x0, waiting for transfers between devices: 112 us -> none  [shards(): chosen = lax.all_gather(local_cols, 'row', axis=0, tiled=True)]
    reduce_scatter x1 -> x0, waiting for transfers between devices: 108 us -> none  [shards(): lax.psum_scatter(partial_value, ('col', 'depth'), scatter_dimension=0, ti...]
    pallas_call x0 -> x1, Pallas kernels: none -> 85.3 us  [run(): pl.pallas_call(functools.partial(kernel, cz, cy), out_shape=(jax.ShapeDty...]
    dot_general x1 -> x0, matrix products: 36.9 us -> none  [shards(): jnp.dot(masked, chosen, precision=lax.Precision.HIGHEST, preferred_elemen...]
    mul x2 -> x0, other arithmetic: 11 us -> none  [the longest x1 10.9 us: shards(): left_blocks * expand(left_pattern[:, 0, :], block, left_blocks.dtype)[:,...]
  transfers between devices with their start and end apart: 2 -> 0, of which waited for: 2 -> 0; matrix products, arithmetic and copies ran while one was open for 5% -> 0% of each run, Pallas kernels for 0% -> 0%
where the time goes in v1:
time: 89.1 us; the launch traced here: 88.2 us
  Pallas kernels  85.3 us (96%)
  local copies, waits for them, and re-layouts  1.92 us (2%)
    pallas_call x1, Pallas kernels, run(): pl.pallas_call(functools.partial(kernel, cz, cy), out_shape=(jax.ShapeDty...  85.3 us

profile of v1, /device:TPU:1, one launch (start us, length us, event | category | flops | bytes accessed | tf_op | source)
XLA Modules:
  0.0 88.2 jit_solution(4554085735388111939)
XLA Ops:
  0.0 0.0 copy-start.1
  0.0 0.0 copy-start.4
  0.0 0.0 copy-start.3
  0.0 0.0 copy-start
  0.0 0.0 copy-start.2
  0.0 85.3 %shard_map.66 = (f32[64,1024]{1,0:T(8,128)S(1)}, s32[8,128]{1,0:T(8,128)}) custom-call(f32[16384,128]{1,0:T(8,128)} %bitcast.5, s32[8,16]{1,0:T(8,128)} %bitcast.9, f32[128,2048]{1,0:T(8,128)} %bitcast.7, s32[1,16]{1,0:T(1,128)} %bitcast.11, s32[8]{0:T(128)} %sub_s.1, f32[64,1024]{1,0:T(8,128)} %sq_v.1), custom_call_target="tpu_custom_call" | custom-call | tf_op jit(solution)/shard_map/pallas_call | solution.py:383
  85.3 1.2 %slice.3 = s32[1,1]{1,0:T(1,128)} slice(s32[8,128]{1,0:T(8,128)} %get-tuple-element.30), slice={[0:1], [0:1]} | slice | bytes 8 | tf_op jit(solution)/shard_map/slice | solution.py:406
  87.2 0.0 copy-done.1
  87.2 0.0 copy-done.4
  87.2 0.0 copy-done.3
  87.2 0.0 copy-done
  87.2 0.0 copy-done.2
  87.2 0.3 conditional.1
  87.5 0.7 copy.12
Async XLA Ops:
  0.0 87.2 %copy-start.1 = (f32[64,1024]{1,0:T(8,128)S(1)}, f32[64,1024]{1,0:T(8,128)}, u32[]{:S(2)}) copy-start(f32[64,1024]{1,0:T(8,128)} %sq_v.1) | copy-start | bytes 786436
  0.0 87.2 %copy-start.4 = (s32[8]{0:T(128)S(1)}, s32[8]{0:T(128)}, u32[]{:S(2)}) copy-start(s32[8]{0:T(128)} %sub_s.1) | copy-start | bytes 100
  0.0 87.2 %copy-start.3 = (s32[1,1,16]{2,1,0:T(1,128)S(1)}, s32[1,1,16]{2,1,0:T(1,128)}, u32[]{:S(2)}) copy-start(s32[1,1,16]{2,1,0:T(1,128)} %param.11) | copy-start | bytes 196
  0.0 87.2 %copy-start = (f32[1,128,2048]{2,1,0:T(8,128)S(1)}, f32[1,128,2048]{2,1,0:T(8,128)}, u32[]{:S(2)}) copy-start(f32[1,128,2048]{2,1,0:T(8,128)} %param.10) | copy-start | bytes 3145732
  0.0 87.2 %copy-start.2 = (s32[8,1,16]{2,1,0:T(1,128)S(1)}, s32[8,1,16]{2,1,0:T(1,128)}, u32[]{:S(2)}) copy-start(s32[8,1,16]{2,1,0:T(1,128)} %param.9) | copy-start | bytes 1540

commit v2 on v1

v2 whole, which is shorter than its diff:
```python
import functools

import jax
import jax.numpy as jnp
from jax import lax
from jax.experimental import pallas as pl
from jax.experimental.pallas import tpu as pltpu
from jax.sharding import PartitionSpec as P

MESH = pl.DeviceIdType.MESH
BS = 128
NH = 4
NW = 8
NR = 16


def dot_nt(a, b):
    return lax.dot_general(a, b, (((1,), (1,)), ((), ())), preferred_element_type=jnp.float32)


def kernel(cz, cy, left_h, lp_h, win_h, rp_h, sub_h, sq_h, out_v, flag_s, *scratch):
    (lp_s, rp_s, sub_s, sq_v, left_v, win_v, ahi, alo, spread, py_v, pz_v, one_v, one_s, idx_v, idx_s, bhi, blo,
     prod, cr, xr, vz, zx, fl_a, fl_b, fl_c, fl_x, fl_z,
     rec0, rec1, rec2, rec3, zr0, zr1, zr2, zr3, yr0, yr1, yr2, yr3,
     ssem, wsem, lsem, py_ss, py_rs, pz_ss, pz_rs, a_ss, a_rs, z_ss, z_rs, y_ss, y_rs, f_ss, f_rs,
     c_ss, c_rs, x_ss, x_rs, v_ss, v_rs, fl_ss, fl_rs) = scratch
    rec = (rec0, rec1, rec2, rec3)
    zr = (zr0, zr1, zr2, zr3)
    yr = (yr0, yr1, yr2, yr3)
    half = cy // 2

    r = lax.axis_index("row")
    x = lax.axis_index("col")
    d = lax.axis_index("depth")
    y = lax.rem(r, 4)
    z = r // 4
    core = lax.rem(d, 2)
    zh = d // 2

    def row_at(dz, dy):
        return lax.rem(z + dz, 4) * 4 + lax.rem(y + dy, 4)

    core_peer = {"depth": d + 1 - 2 * core}
    zh_peer = {"depth": lax.rem(d + 2, 4)}

    def x_peer(dx):
        return {"col": lax.rem(x + dx, 4)}

    def remote(src, dst, ss, rs, device):
        return pltpu.make_async_remote_copy(
            src_ref=src, dst_ref=dst, send_sem=ss, recv_sem=rs, device_id=device, device_id_type=MESH
        )

    barrier = pltpu.get_barrier_semaphore()
    for k in range(1, 4):
        pl.semaphore_signal(barrier, inc=1, device_id={"row": row_at(0, k)}, device_id_type=MESH)
        pl.semaphore_signal(barrier, inc=1, device_id={"row": row_at(k, 0)}, device_id_type=MESH)
        pl.semaphore_signal(barrier, inc=1, device_id=x_peer(k), device_id_type=MESH)
    pl.semaphore_signal(barrier, inc=1, device_id=core_peer, device_id_type=MESH)
    pl.semaphore_signal(barrier, inc=1, device_id=zh_peer, device_id_type=MESH)

    small = []
    for k, (src, dst) in enumerate(((sub_h, sub_s), (rp_h, rp_s), (lp_h, lp_s), (sq_h, sq_v))):
        cp = pltpu.make_async_copy(src, dst, ssem.at[k])
        cp.start()
        small.append(cp)
    win_copies = []
    for w in range(16):
        cp = pltpu.make_async_copy(win_h.at[:, pl.ds(w * BS, BS)], win_v.at[w], wsem.at[w])
        cp.start()
        win_copies.append(cp)
    left_copies = []
    for part in range(4):
        cp = pltpu.make_async_copy(
            left_h.at[pl.ds(part * 4096, 4096)], left_v.at[pl.ds(part * 4096, 4096)], lsem.at[1 + part]
        )
        cp.start()
        left_copies.append(cp)
    for cp in small:
        cp.wait()

    lane = lax.broadcasted_iota(jnp.int32, (8, 128), 1)
    mine = jnp.zeros((8, 128), jnp.int32)
    for w in range(NW):
        mine = jnp.where(lane == y * NW + w, rp_s[0, sub_s[w]], mine)
    py_v[y] = mine
    for cp in win_copies:
        cp.wait()
    for w in range(NW):
        block = win_v[sub_s[w]].T
        for h in range(NH):
            for to in range(4):
                at = 32 * h + 8 * to
                spread[h, to, w] = block[at:at + 8, :]
    pl.semaphore_wait(barrier, 11)

    pt = []
    for dy in (1, 3, 2):
        cp = remote(py_v.at[y], py_v.at[y], py_ss.at[dy], py_rs.at[dy], {"row": row_at(0, dy)})
        cp.start()
        pt.append(cp)

    a2a = []
    for h in range(NH):
        row = []
        for dy in (1, 3, 2):
            to = lax.rem(y + dy, 4)
            cp = remote(spread.at[h, to], rec[h].at[pl.ds(y * NW, NW)], a_ss.at[h, dy], a_rs.at[h, dy], {"row": row_at(0, dy)})
            cp.start()
            row.append(cp)
        a2a.append(row)
        rec[h][pl.ds(y * NW, NW)] = spread[h, y]

    def prepare():
        for cp in left_copies:
            cp.wait()

        def body(piece, _):
            at = lax.rem(piece, 2) * 512 + lax.rem(piece // 2, 2) * 256 + (piece // 4) * 64
            at = pl.multiple_of(at, 64)
            for q in range(NR):
                v = left_v[pl.ds(piece * 1024 + q, 64, stride=16), :]
                v = jnp.where(jnp.full((64, 128), lp_s[piece // 2, q], jnp.int32) != 0, v, 0.0)
                hi = v.astype(jnp.bfloat16)
                ahi[pl.ds(at, 64), q * BS:(q + 1) * BS] = hi
                alo[pl.ds(at, 64), q * BS:(q + 1) * BS] = (v - hi.astype(jnp.float32)).astype(jnp.bfloat16)
            return 0

        lax.fori_loop(0, 16, body, 0)

    def column(v):
        return jnp.broadcast_to(v[0:1, :], (128, 128)).T

    for cp in pt:
        cp.wait_recv()
    pool = (py_v[0] + py_v[1]) + (py_v[2] + py_v[3])
    pz_v[z] = pool
    for dz in (1, 3, 2):
        cp = remote(pz_v.at[z], pz_v.at[z], pz_ss.at[dz], pz_rs.at[dz], {"row": row_at(dz, 0)})
        cp.start()
        pt.append(cp)
    upto = pool
    for s in (1, 2, 4, 8, 16):
        upto = upto + jnp.where(lane >= s, pltpu.roll(upto, s, 1), 0)
    blk = lax.broadcasted_iota(jnp.int32, (32, 128), 0)
    slot = lax.broadcasted_iota(jnp.int32, (32, 128), 1)
    first = jnp.where((column(pool)[0:32, :] != 0) & (column(upto - pool)[0:32, :] == slot), blk, 0)
    one_v[...] = jnp.broadcast_to(jnp.sum(first, axis=0, keepdims=True), (8, 128))
    to_one = pltpu.make_async_copy(one_v, one_s, lsem.at[0])
    to_one.start()
    to_one.wait()

    zg = []
    for h in range(NH):
        for cp in a2a[h]:
            cp.wait_recv()

        def pack(j, _, h=h):
            at = one_s[0, j]
            zr[h][z * cz + j] = rec[h][at]
            return 0

        if cz <= 20:
            for j in range(cz):
                pack(j, 0)
        else:
            lax.fori_loop(0, cz, pack, 0)
        row = {}
        part = zr[h].at[pl.ds(z * cz, cz)]
        for dz in (2, 1, 3):
            row[dz] = remote(part, part, z_ss.at[h, dz], z_rs.at[h, dz], {"row": row_at(dz, 0)})
        row[2].start()

        @pl.when(z != 3)
        def _(cp=row[1]):
            cp.start()

        @pl.when(z != 0)
        def _(cp=row[3]):
            cp.start()

        zg.append(row)

    for cp in pt[3:]:
        cp.wait_recv()
    pat = jnp.where(lane < 32, pz_v[0], 0)
    for k in range(1, 4):
        pat = jnp.where(lane // 32 == k, pltpu.roll(pz_v[k], 32 * k, 1), pat)
    in_pool = lax.rem(lane, 32)
    c32 = pat
    for s in (1, 2, 4, 8, 16):
        c32 = c32 + jnp.where(in_pool >= s, pltpu.roll(c32, s, 1), 0)
    call = pat
    for s in (1, 2, 4, 8, 16, 32, 64):
        call = call + jnp.where(lane >= s, pltpu.roll(call, s, 1), 0)
    rank = call - pat
    zsrc = (lane // 32) * cz + jnp.minimum(c32 - pat, cz - 1)
    slot = lax.broadcasted_iota(jnp.int32, (128, 128), 1)
    second = jnp.where((column(pat) != 0) & (column(rank) == slot), column(zsrc), 0)
    idx_v[0:2, :] = pat[0:2, :]
    idx_v[1:2, :] = jnp.sum(second, axis=0, keepdims=True)
    idx_v[2:3, :] = jnp.minimum(rank, cy - 1)[0:1, :]
    idx_v[3:4, :] = pat[0:1, :]
    idx_v[4:8, :] = pat[0:4, :]
    over = jnp.where((in_pool == 31) & (c32 > cz), 1, 0) + jnp.where((lane == 127) & (call > cy), 1, 0)
    for s in (1, 2, 4, 8, 16, 32, 64):
        over = over + pltpu.roll(over, s, 1)
    fl_a[...] = over
    to_s = pltpu.make_async_copy(idx_v, idx_s, lsem.at[5])
    to_s.start()
    to_s.wait()

    zf = []
    for h in range(NH):
        up = zr[h].at[pl.ds(0, cz)]
        down = zr[h].at[pl.ds(3 * cz, cz)]
        zf.append((
            remote(up, up, z_ss.at[h, 0], z_rs.at[h, 3], {"row": 12 + y}),
            remote(down, down, z_ss.at[h, 0], z_rs.at[h, 1], {"row": y}),
        ))

    def z_forward(h):
        zg[h][2].wait_recv()

        @pl.when(z == 2)
        def _():
            zf[h][0].start()

        @pl.when(z == 1)
        def _():
            zf[h][1].start()

    sides = ((0, 1), (1, 3))

    def yg(h, side, k):
        part = yr[h].at[y, pl.ds(k * half, half)]
        return remote(part, part, y_ss.at[h, side, k], y_rs.at[h, side, k], {"row": row_at(0, sides[side][1])})

    def fg(h, side):
        part = yr[h].at[lax.rem(y + (3 if side == 0 else 1), 4), pl.ds(side * half, half)]
        return remote(part, part, f_ss.at[h, side], f_rs.at[h, side], {"row": row_at(0, sides[side][1])})

    def y_send(h):
        zg[h][1].wait_recv()
        zg[h][3].wait_recv()

        def pack(j, _):
            at = idx_s[1, j]
            yr[h][y, j] = zr[h][at]
            return 0

        if cy <= 64:
            def ten(i, _):
                for k in range(10):
                    pack(i * 10 + k, 0)
                return 0

            lax.fori_loop(0, cy // 10, ten, 0)
        else:
            lax.fori_loop(0, cy, pack, 0)
        for side in (0, 1):
            for k in ((0, 1) if side == 0 else (1, 0)):
                yg(h, side, k).start()

    def y_forward(h):
        for side in (0, 1):
            yg(h, side, side).wait_recv()
            fg(h, side).start()

    def y_wait(h):
        for side in (0, 1):
            yg(h, side, 1 - side).wait_recv()
            fg(h, side).wait_recv()

    def expand(h):
        def body(w, _):
            at = pl.multiple_of(w * 32, 32)
            for q in range(NR):
                place = idx_s[2, q * NW + w]
                keep = jnp.full((32, 128), idx_s[3, q * NW + w], jnp.int32) != 0
                v = jnp.concatenate([yr[h][k, place] for k in range(4)], axis=0)
                v = jnp.where(keep, v, 0.0)
                hi = v.astype(jnp.bfloat16)
                bhi[pl.ds(at, 32), q * BS:(q + 1) * BS] = hi
                blo[pl.ds(at, 32), q * BS:(q + 1) * BS] = (v - hi.astype(jnp.float32)).astype(jnp.bfloat16)
            return 0

        lax.fori_loop(0, NW, body, 0)

    def product(s):
        swap_core = 1 - lax.rem(s, 2)
        swap_zh = 1 - lax.rem(s // 2, 2)
        core_to = core + swap_core * (1 - 2 * core)
        zh_to = zh + swap_zh * (1 - 2 * zh)
        at = pl.multiple_of(core_to * 512 + zh_to * 256, 256)
        a_hi, a_lo = ahi[pl.ds(at, 256), :], alo[pl.ds(at, 256), :]
        b_hi, b_lo = bhi[...], blo[...]
        return dot_nt(a_hi, b_hi) + dot_nt(a_hi, b_lo) + dot_nt(a_lo, b_hi)

    def cg(h, p):
        return remote(prod.at[4 * h + 2 * p], cr.at[h, p], c_ss.at[h, p], c_rs.at[h, p], core_peer)

    def xg(h, p, dx):
        part = prod.at[4 * h + 2 * p + 1, pl.ds(pl.multiple_of(lax.rem(x + dx, 4) * 64, 64), 64)]
        return remote(part, xr.at[h, p, dx - 1], x_ss.at[h, p, dx], x_rs.at[h, p, dx], x_peer(dx))

    def vg(h):
        return remote(vz.at[h, 0], zx.at[h], v_ss.at[h], v_rs.at[h], zh_peer)

    def flg(k):
        if k == 0:
            return remote(fl_a, fl_c, fl_ss.at[0], fl_rs.at[0], core_peer)
        if k == 4:
            return remote(fl_b.at[1], fl_z, fl_ss.at[4], fl_rs.at[4], zh_peer)
        return remote(fl_b.at[0], fl_x.at[k - 1], fl_ss.at[k], fl_rs.at[k], x_peer(k))

    def to_core(h, p):
        cg(h, p).start()
        if (h, p) == (0, 0):
            flg(0).start()

    def over_x(h, p):
        cg(h, p).wait_recv()
        prod[4 * h + 2 * p + 1] = prod[4 * h + 2 * p + 1] + cr[h, p]
        for dx in (2, 1, 3):
            xg(h, p, dx).start()
        if (h, p) == (0, 0):
            flg(0).wait_recv()
            fl_b[0] = fl_a[...] + fl_c[...]
            for dx in (1, 3, 2):
                flg(dx).start()

    def sum_x(h, p):
        total = prod[4 * h + 2 * p + 1, pl.ds(pl.multiple_of(x * 64, 64), 64), :]
        for dx in (1, 3, 2):
            xg(h, p, dx).wait_recv()
            total = total + xr[h, p, dx - 1]
        vz[h, p] = total

    def over_zh(h):
        sum_x(h, 0)
        vg(h).start()
        if h == 0:
            for dx in (1, 3, 2):
                flg(dx).wait_recv()
            fl_b[1] = (fl_b[0] + fl_x[0]) + (fl_x[1] + fl_x[2])
            flg(4).start()

    lane64 = lax.broadcasted_iota(jnp.int32, (64, 128), 1)

    def finish(h):
        vg(h).wait_recv()
        total = vz[h, 1] + zx[h]
        for w in range(NW):
            tile = total[:, (w // 4) * 128:(w // 4 + 1) * 128]
            shift = (32 * h - 32 * (w % 4)) % 128
            if shift:
                tile = pltpu.roll(tile, shift, 1)
            cols = slice(w * BS, (w + 1) * BS)
            value = 3.0 * sq_v[:, cols] - 2.0 * tile
            if h:
                value = jnp.where(lane64 // 32 == h, value, out_v[:, cols])
            out_v[:, cols] = value
        if h == 0:
            flg(4).wait_recv()
            one_v[...] = fl_b[1] + fl_z[...]
            to_flag = pltpu.make_async_copy(one_v, one_s, lsem.at[0])
            to_flag.start()
            to_flag.wait()
            flag_s[0, 0] = one_s[0, 0]

    prepare()
    z_forward(0)
    y_send(0)
    z_forward(1)
    y_forward(0)
    y_send(1)

    def step(s, _):
        for h in range(NH):
            @pl.when(s == 4 * h)
            def _(h=h):
                y_wait(h)
                expand(h)

        prod[s] = product(s)

        for h in range(NH):
            @pl.when(s == 4 * h)
            def _(h=h):
                to_core(h, 0)
                if h + 1 < NH:
                    y_forward(h + 1)
                if h + 2 < NH:
                    z_forward(h + 2)
                    y_send(h + 2)

            @pl.when(s == 4 * h + 1)
            def _(h=h):
                over_x(h, 0)

            @pl.when(s == 4 * h + 2)
            def _(h=h):
                to_core(h, 1)
                if h >= 1:
                    over_zh(h - 1)

            @pl.when(s == 4 * h + 3)
            def _(h=h):
                if h >= 1:
                    sum_x(h - 1, 1)
                over_x(h, 1)
                if h >= 2:
                    finish(h - 2)

        return 0

    lax.fori_loop(0, 4 * NH, step, 0)
    over_zh(NH - 1)
    sum_x(NH - 1, 1)
    finish(NH - 2)
    finish(NH - 1)

    for cp in pt:
        cp.wait_send()
    for row in a2a:
        for cp in row:
            cp.wait_send()
    for row in zg:
        row[2].wait_send()

    @pl.when(z != 3)
    def _():
        for row in zg:
            row[1].wait_send()

    @pl.when(z != 0)
    def _():
        for row in zg:
            row[3].wait_send()

    @pl.when(z == 2)
    def _():
        for row in zf:
            row[0].wait_send()

    @pl.when(z == 1)
    def _():
        for row in zf:
            row[1].wait_send()

    for h in range(NH):
        for side in (0, 1):
            fg(h, side).wait_send()
            for k in (0, 1):
                yg(h, side, k).wait_send()
        for p in (0, 1):
            cg(h, p).wait_send()
            for dx in (1, 2, 3):
                xg(h, p, dx).wait_send()
        vg(h).wait_send()
    for k in range(5):
        flg(k).wait_send()


def run(cz, cy, collective_id, left, lp, win, rp, sub, sq):
    any_ = pl.BlockSpec(memory_space=pl.ANY)
    vmem = pl.BlockSpec(memory_space=pltpu.VMEM)
    smem = pl.BlockSpec(memory_space=pltpu.SMEM)
    f32, bf16, i32 = jnp.float32, jnp.bfloat16, jnp.int32
    dma = pltpu.SemaphoreType.DMA
    scratch = [
        pltpu.SMEM((8, NR), i32),
        pltpu.SMEM((1, 16), i32),
        pltpu.SMEM((8,), i32),
        pltpu.VMEM((64, 1024), f32),
        pltpu.VMEM((16384, 128), f32),
        pltpu.VMEM((16, 128, 128), f32),
        pltpu.VMEM((1024, 2048), bf16),
        pltpu.VMEM((1024, 2048), bf16),
        pltpu.VMEM((NH, 4, NW, 8, 128), f32),
        pltpu.VMEM((4, 8, 128), i32),
        pltpu.VMEM((4, 8, 128), i32),
        pltpu.VMEM((8, 128), i32),
        pltpu.SMEM((8, 128), i32),
        pltpu.VMEM((8, 128), i32),
        pltpu.SMEM((8, 128), i32),
        pltpu.VMEM((256, 2048), bf16),
        pltpu.VMEM((256, 2048), bf16),
        pltpu.VMEM((4 * NH, 256, 256), f32),
        pltpu.VMEM((NH, 2, 256, 256), f32),
        pltpu.VMEM((NH, 2, 3, 64, 256), f32),
        pltpu.VMEM((NH, 2, 64, 256), f32),
        pltpu.VMEM((NH, 64, 256), f32),
        pltpu.VMEM((8, 128), i32),
        pltpu.VMEM((2, 8, 128), i32),
        pltpu.VMEM((8, 128), i32),
        pltpu.VMEM((3, 8, 128), i32),
        pltpu.VMEM((8, 128), i32),
    ]
    scratch += [pltpu.VMEM((4 * NW, 8, 128), f32) for _ in range(NH)]
    scratch += [pltpu.VMEM((4 * cz, 8, 128), f32) for _ in range(NH)]
    scratch += [pltpu.VMEM((4, cy, 8, 128), f32) for _ in range(NH)]
    scratch += [
        dma((4,)), dma((16,)), dma((6,)),
        dma((4,)), dma((4,)), dma((4,)), dma((4,)),
        dma((NH, 4)), dma((NH, 4)),
        dma((NH, 4)), dma((NH, 4)),
        dma((NH, 2, 2)), dma((NH, 2, 2)),
        dma((NH, 2)), dma((NH, 2)),
        dma((NH, 2)), dma((NH, 2)),
        dma((NH, 2, 4)), dma((NH, 2, 4)),
        dma((NH,)), dma((NH,)),
        dma((5,)), dma((5,)),
    ]
    return pl.pallas_call(
        functools.partial(kernel, cz, cy),
        out_shape=(jax.ShapeDtypeStruct((64, 1024), f32), jax.ShapeDtypeStruct((1, 1), i32)),
        in_specs=[any_] * 6,
        out_specs=(vmem, smem),
        scratch_shapes=scratch,
        compiler_params=pltpu.CompilerParams(
            collective_id=collective_id, has_side_effects=True, vmem_limit_bytes=56 * 2**20
        ),
    )(left, lp, win, rp, sub, sq)


def shards(left_blocks, left_pattern, right_window, right_pattern, subset_cols, square_cols):
    args = (
        left_blocks.reshape(1024 * NR, BS),
        left_pattern.reshape(8, NR),
        right_window.reshape(128, 2048),
        right_pattern.reshape(1, 16),
        subset_cols,
        square_cols,
    )
    fast, flag = run(18, 50, 0, *args)
    return lax.cond(
        flag[0, 0] > 0,
        lambda value, *rest: run(32, 128, 1, *rest)[0],
        lambda value, *rest: value,
        fast, *args,
    )


def solution(mesh):
    return jax.shard_map(
        shards,
        mesh=mesh,
        in_specs=(
            P("row", ("col", "depth"), None),
            P("row", ("col", "depth"), None),
            P(("col", "depth"), "row", None),
            P(("col", "depth"), "row", None),
            P(),
            P(("row", "col", "depth"), None),
        ),
        out_specs=P(("row", "col", "depth"), None),
        check_vma=False,
    )
```

time: 89.1 us -> 77.4 us (0.87)
  Pallas kernels: 85.3 us -> 75.9 us
  local copies, waits for them, and re-layouts: 1.92 us -> 0.72 us
    pallas_call x1, Pallas kernels: 85.3 us -> 75.9 us  [run(): pl.pallas_call(functools.partial(kernel, cz, cy), out_shape=(jax.ShapeDty...]
    slice x1 -> x0, local copies, waits for them, and re-layouts: 1.2 us -> none  [shards(): flag[0, 0] > 0]
where the time goes in v2:
time: 77.4 us; the launch traced here: 77.3 us
  Pallas kernels  75.9 us (98%)
    pallas_call x1, Pallas kernels, run(): pl.pallas_call(functools.partial(kernel, cz, cy), out_shape=(jax.ShapeDty...  75.9 us

profile of v2, /device:TPU:1, one launch (start us, length us, event | category | flops | bytes accessed | tf_op | source)
XLA Modules:
  0.0 77.3 jit_solution(2237333140363933501)
XLA Ops:
  0.0 0.0 copy-start.1
  0.0 0.0 copy-start.4
  0.0 0.0 copy-start.3
  0.0 0.0 copy-start
  0.0 0.0 copy-start.2
  0.0 75.9 %shard_map.66 = (f32[64,1024]{1,0:T(8,128)S(1)}, s32[1,1]{1,0:T(1,128)}) custom-call(f32[16384,128]{1,0:T(8,128)} %bitcast.5, s32[8,16]{1,0:T(8,128)} %bitcast.9, f32[128,2048]{1,0:T(8,128)} %bitcast.7, s32[1,16]{1,0:T(1,128)} %bitcast.11, s32[8]{0:T(128)} %sub_h.1, f32[64,1024]{1,0:T(8,128)} %sq_h.1), custom_call_target="tpu_custom_call" | custom-call | tf_op jit(solution)/shard_map/pallas_call | solution.py:516
  76.6 0.0 copy-done.1
  76.6 0.0 copy-done.4
  76.6 0.0 copy-done.3
  76.6 0.0 copy-done
  76.6 0.0 copy-done.2
  76.6 0.7 copy.12
  (1 shorter events, 0.0 us)
Async XLA Ops:
  0.0 76.6 %copy-start.1 = (f32[64,1024]{1,0:T(8,128)S(1)}, f32[64,1024]{1,0:T(8,128)}, u32[]{:S(2)}) copy-start(f32[64,1024]{1,0:T(8,128)} %sq_h.1) | copy-start | bytes 786436
  0.0 76.6 %copy-start.4 = (s32[8]{0:T(128)S(1)}, s32[8]{0:T(128)}, u32[]{:S(2)}) copy-start(s32[8]{0:T(128)} %sub_h.1) | copy-start | bytes 100
  0.0 76.6 %copy-start.3 = (s32[1,1,16]{2,1,0:T(1,128)S(1)}, s32[1,1,16]{2,1,0:T(1,128)}, u32[]{:S(2)}) copy-start(s32[1,1,16]{2,1,0:T(1,128)} %param.11) | copy-start | bytes 196
  0.0 76.6 %copy-start = (f32[1,128,2048]{2,1,0:T(8,128)S(1)}, f32[1,128,2048]{2,1,0:T(8,128)}, u32[]{:S(2)}) copy-start(f32[1,128,2048]{2,1,0:T(8,128)} %param.10) | copy-start | bytes 3145732
  0.0 76.6 %copy-start.2 = (s32[8,1,16]{2,1,0:T(1,128)S(1)}, s32[8,1,16]{2,1,0:T(1,128)}, u32[]{:S(2)}) copy-start(s32[8,1,16]{2,1,0:T(1,128)} %param.9) | copy-start | bytes 1540

commit v3 on v2

--- a/solution.py
+++ b/solution.py
@@ -111,8 +111,8 @@
         a2a.append(row)
         rec[h][pl.ds(y * NW, NW)] = spread[h, y]
 
-    def prepare():
-        for cp in left_copies:
+    def prepare(first):
+        for cp in left_copies[first // 4:first // 4 + 2]:
             cp.wait()
 
         def body(piece, _):
@@ -126,7 +126,7 @@
                 alo[pl.ds(at, 64), q * BS:(q + 1) * BS] = (v - hi.astype(jnp.float32)).astype(jnp.bfloat16)
             return 0
 
-        lax.fori_loop(0, 16, body, 0)
+        lax.fori_loop(first, first + 8, body, 0)
 
     def column(v):
         return jnp.broadcast_to(v[0:1, :], (128, 128)).T
@@ -144,7 +144,8 @@
         upto = upto + jnp.where(lane >= s, pltpu.roll(upto, s, 1), 0)
     blk = lax.broadcasted_iota(jnp.int32, (32, 128), 0)
     slot = lax.broadcasted_iota(jnp.int32, (32, 128), 1)
-    first = jnp.where((column(pool)[0:32, :] != 0) & (column(upto - pool)[0:32, :] == slot), blk, 0)
+    place = jnp.where(pool != 0, upto - pool, 255)
+    first = jnp.where(column(place)[0:32, :] == slot, blk, 0)
     one_v[...] = jnp.broadcast_to(jnp.sum(first, axis=0, keepdims=True), (8, 128))
     to_one = pltpu.make_async_copy(one_v, one_s, lsem.at[0])
     to_one.start()
@@ -196,7 +197,7 @@
     rank = call - pat
     zsrc = (lane // 32) * cz + jnp.minimum(c32 - pat, cz - 1)
     slot = lax.broadcasted_iota(jnp.int32, (128, 128), 1)
-    second = jnp.where((column(pat) != 0) & (column(rank) == slot), column(zsrc), 0)
+    second = jnp.where(column(jnp.where(pat != 0, rank, 255)) == slot, column(zsrc), 0)
     idx_v[0:2, :] = pat[0:2, :]
     idx_v[1:2, :] = jnp.sum(second, axis=0, keepdims=True)
     idx_v[2:3, :] = jnp.minimum(rank, cy - 1)[0:1, :]
@@ -369,9 +370,10 @@
             to_flag.wait()
             flag_s[0, 0] = one_s[0, 0]
 
-    prepare()
+    prepare(0)
     z_forward(0)
     y_send(0)
+    prepare(8)
     z_forward(1)
     y_forward(0)
     y_send(1)
@@ -407,18 +409,22 @@
 
             @pl.when(s == 4 * h + 3)
             def _(h=h):
-                if h >= 1:
-                    sum_x(h - 1, 1)
-                over_x(h, 1)
-                if h >= 2:
-                    finish(h - 2)
+                if h + 1 < NH:
+                    if h >= 1:
+                        sum_x(h - 1, 1)
+                    over_x(h, 1)
+                    if h >= 2:
+                        finish(h - 2)
 
         return 0
 
     lax.fori_loop(0, 4 * NH, step, 0)
+    over_x(NH - 1, 1)
     over_zh(NH - 1)
+    sum_x(NH - 2, 1)
+    finish(NH - 3)
+    finish(NH - 2)
     sum_x(NH - 1, 1)
-    finish(NH - 2)
     finish(NH - 1)
 
     for cp in pt:

time: 77.4 us -> 76.6 us (0.990)
  Pallas kernels: 75.9 us -> 75 us
    pallas_call x1, Pallas kernels: 75.9 us -> 75 us  [run(): pl.pallas_call(functools.partial(kernel, cz, cy), out_shape=(jax.ShapeDty...]
where the time goes in v3:
time: 76.6 us; the launch traced here: 76.5 us
  Pallas kernels  75 us (98%)
    pallas_call x1, Pallas kernels, run(): pl.pallas_call(functools.partial(kernel, cz, cy), out_shape=(jax.ShapeDty...  75 us

profile of v3, /device:TPU:1, one launch (start us, length us, event | category | flops | bytes accessed | tf_op | source)
XLA Modules:
  0.0 76.5 jit_solution(8087309363155862774)
XLA Ops:
  0.0 0.0 copy-start.1
  0.0 0.0 copy-start.4
  0.0 0.0 copy-start.3
  0.0 0.0 copy-start
  0.0 0.0 copy-start.2
  0.0 75.0 %shard_map.66 = (f32[64,1024]{1,0:T(8,128)S(1)}, s32[1,1]{1,0:T(1,128)}) custom-call(f32[16384,128]{1,0:T(8,128)} %bitcast.5, s32[8,16]{1,0:T(8,128)} %bitcast.9, f32[128,2048]{1,0:T(8,128)} %bitcast.7, s32[1,16]{1,0:T(1,128)} %bitcast.11, s32[8]{0:T(128)} %sub_h.1, f32[64,1024]{1,0:T(8,128)} %sq_h.1), custom_call_target="tpu_custom_call" | custom-call | tf_op jit(solution)/shard_map/pallas_call | solution.py:522
  75.7 0.0 copy-done.1
  75.7 0.0 copy-done.4
  75.8 0.0 copy-done.3
  75.8 0.0 copy-done
  75.8 0.0 copy-done.2
  75.8 0.7 copy.12
  (1 shorter events, 0.0 us)
Async XLA Ops:
  0.0 75.7 %copy-start.1 = (f32[64,1024]{1,0:T(8,128)S(1)}, f32[64,1024]{1,0:T(8,128)}, u32[]{:S(2)}) copy-start(f32[64,1024]{1,0:T(8,128)} %sq_h.1) | copy-start | bytes 786436
  0.0 75.7 %copy-start.4 = (s32[8]{0:T(128)S(1)}, s32[8]{0:T(128)}, u32[]{:S(2)}) copy-start(s32[8]{0:T(128)} %sub_h.1) | copy-start | bytes 100
  0.0 75.8 %copy-start.3 = (s32[1,1,16]{2,1,0:T(1,128)S(1)}, s32[1,1,16]{2,1,0:T(1,128)}, u32[]{:S(2)}) copy-start(s32[1,1,16]{2,1,0:T(1,128)} %param.11) | copy-start | bytes 196
  0.0 75.8 %copy-start = (f32[1,128,2048]{2,1,0:T(8,128)S(1)}, f32[1,128,2048]{2,1,0:T(8,128)}, u32[]{:S(2)}) copy-start(f32[1,128,2048]{2,1,0:T(8,128)} %param.10) | copy-start | bytes 3145732
  0.0 75.8 %copy-start.2 = (s32[8,1,16]{2,1,0:T(1,128)S(1)}, s32[8,1,16]{2,1,0:T(1,128)}, u32[]{:S(2)}) copy-start(s32[8,1,16]{2,1,0:T(1,128)} %param.9) | copy-start | bytes 1540

commit v4 on v3

--- a/solution.py
+++ b/solution.py
@@ -103,7 +103,7 @@
     a2a = []
     for h in range(NH):
         row = []
-        for dy in (1, 3, 2):
+        for dy in (2, 1, 3):
             to = lax.rem(y + dy, 4)
             cp = remote(spread.at[h, to], rec[h].at[pl.ds(y * NW, NW)], a_ss.at[h, dy], a_rs.at[h, dy], {"row": row_at(0, dy)})
             cp.start()

time: 76.6 us -> 76.6 us (level)
  no operation moved by 1% of the time
where the time goes in v4:
time: 76.6 us
  Pallas kernels  75.1 us (98%)
    pallas_call x1, Pallas kernels, run(): pl.pallas_call(functools.partial(kernel, cz, cy), out_shape=(jax.ShapeDty...  75.1 us

profile of v4, /device:TPU:1, one launch (start us, length us, event | category | flops | bytes accessed | tf_op | source)
XLA Modules:
  0.0 76.6 jit_solution(80061672350956587)
XLA Ops:
  0.0 0.0 copy-start.1
  0.0 0.0 copy-start.4
  0.0 0.0 copy-start.3
  0.0 0.0 copy-start
  0.0 0.0 copy-start.2
  0.0 75.1 %shard_map.66 = (f32[64,1024]{1,0:T(8,128)S(1)}, s32[1,1]{1,0:T(1,128)}) custom-call(f32[16384,128]{1,0:T(8,128)} %bitcast.5, s32[8,16]{1,0:T(8,128)} %bitcast.9, f32[128,2048]{1,0:T(8,128)} %bitcast.7, s32[1,16]{1,0:T(1,128)} %bitcast.11, s32[8]{0:T(128)} %sub_h.1, f32[64,1024]{1,0:T(8,128)} %sq_h.1), custom_call_target="tpu_custom_call" | custom-call | tf_op jit(solution)/shard_map/pallas_call | solution.py:522
  75.8 0.0 copy-done.1
  75.8 0.0 copy-done.4
  75.8 0.0 copy-done.3
  75.8 0.0 copy-done
  75.8 0.0 copy-done.2
  75.8 0.7 copy.12
  (1 shorter events, 0.0 us)
Async XLA Ops:
  0.0 75.8 %copy-start.1 = (f32[64,1024]{1,0:T(8,128)S(1)}, f32[64,1024]{1,0:T(8,128)}, u32[]{:S(2)}) copy-start(f32[64,1024]{1,0:T(8,128)} %sq_h.1) | copy-start | bytes 786436
  0.0 75.8 %copy-start.4 = (s32[8]{0:T(128)S(1)}, s32[8]{0:T(128)}, u32[]{:S(2)}) copy-start(s32[8]{0:T(128)} %sub_h.1) | copy-start | bytes 100
  0.0 75.8 %copy-start.3 = (s32[1,1,16]{2,1,0:T(1,128)S(1)}, s32[1,1,16]{2,1,0:T(1,128)}, u32[]{:S(2)}) copy-start(s32[1,1,16]{2,1,0:T(1,128)} %param.11) | copy-start | bytes 196
  0.0 75.8 %copy-start = (f32[1,128,2048]{2,1,0:T(8,128)S(1)}, f32[1,128,2048]{2,1,0:T(8,128)}, u32[]{:S(2)}) copy-start(f32[1,128,2048]{2,1,0:T(8,128)} %param.10) | copy-start | bytes 3145732
  0.0 75.8 %copy-start.2 = (s32[8,1,16]{2,1,0:T(1,128)S(1)}, s32[8,1,16]{2,1,0:T(1,128)}, u32[]{:S(2)}) copy-start(s32[8,1,16]{2,1,0:T(1,128)} %param.9) | copy-start | bytes 1540
